TPU v7x, 128 devices: a whole 4x4x4 slice. The times are simulated.
128 devices in a mesh: gx: 8 (over x, z_hi), gy: 16 (over y, z_lo, core).
Axes of the slice: x: 4, y: 4, z: 4 (z_hi: 2, z_lo: 2; z = z_hi * 2 + z_lo), core: 2. Of those that a mesh axis runs over, the one named last changes fastest.
Arguments:
- weights: float32 [1048576, 128], P(('gx', 'gy')), may hold values from -0.625 to 0.625
- phases: float32 [7, 524288, 128], P(None, ('gx', 'gy')), may hold values from -3.140625 to 3.140625
Outputs:
- result: float32 [1048576, 128], P(('gx', 'gy'))
All inputs are finite; a program needn't handle non-finite values.
Results may differ from a plain program's by a relative error of at most 0.00012.
Values sent between devices are 32-bit elements; how exact they have to be, the bound alone decides.
A program may use at most 192 MiB of HBM per device.

v0:
```python
import math

import jax
import jax.numpy as jnp
from jax import lax
from jax.sharding import PartitionSpec as P


def from_partner(block, axis, bit):
    count = lax.axis_size(axis)
    route = []
    for low in range(count):
        high = low | 1 << bit
        if high != low and high < count:
            route += [(low, high), (high, low)]
    return lax.ppermute(block, axis, route)


def level_matrices():
    node_index = jnp.arange(8, dtype=jnp.float32)
    cheb_nodes = jnp.cos((2.0 * node_index + 1.0) * math.pi / 16.0)
    eye_side = jnp.eye(8, dtype=jnp.float32)
    eye_pair = jnp.eye(2, dtype=jnp.float32)
    diagonal_mask = jnp.arange(8)[:, None, None] == jnp.arange(8)[None, None, :]
    along_one = []
    along_two = []
    for child_index in range(2):
        points = (cheb_nodes + (2.0 * child_index - 1.0)) * 0.5
        numerators = points[None, :, None] - cheb_nodes[None, None, :]
        denominators = cheb_nodes[:, None, None] - cheb_nodes[None, None, :]
        factor = jnp.where(
            diagonal_mask, 1.0, numerators / jnp.where(diagonal_mask, 1.0, denominators)
        )
        lagrange = jnp.prod(factor, axis=2)
        along_one.append(jnp.kron(eye_pair, jnp.kron(lagrange, eye_side)))
        along_two.append(jnp.kron(eye_pair, jnp.kron(eye_side, lagrange)))
    return (jnp.concatenate(along_one, axis=1), jnp.concatenate(along_two, axis=1))


def modulate(values, angle_rows):
    rank_size = angle_rows.shape[-1]
    real_part = values[..., :rank_size]
    imag_part = values[..., rank_size:]
    cosine = jnp.cos(angle_rows)
    sine_part = jnp.sin(angle_rows)
    return jnp.concatenate(
        [cosine * real_part - sine_part * imag_part, sine_part * real_part + cosine * imag_part],
        axis=-1,
    )


def interpolate(rows, level_matrix):
    return jnp.dot(
        rows, level_matrix, precision=lax.Precision.HIGHEST, preferred_element_type=jnp.float32
    )


def level_step(current, angle_rows, level_matrix, own_bit, bit_pos, along_x):
    row_count = current.shape[0]
    half_rows = row_count // 2
    modulated = modulate(current, angle_rows)
    kept_rows = lax.dynamic_slice_in_dim(modulated, own_bit * half_rows, half_rows, 0)
    sent_rows = lax.dynamic_slice_in_dim(modulated, (1 - own_bit) * half_rows, half_rows, 0)
    if along_x:
        arrived = from_partner(sent_rows, "gx", bit_pos)
    else:
        arrived = from_partner(sent_rows, "gy", bit_pos)
    joined = interpolate(kept_rows + arrived, level_matrix)
    return joined.reshape(row_count, current.shape[1])


def shards(weights, phases):
    row_count = weights.shape[0]
    rank_size = weights.shape[1] // 2
    angles = phases.reshape(phases.shape[0], row_count, rank_size)
    matrices = level_matrices()
    x_bits = lax.axis_size("gx").bit_length() - 1
    y_bits = lax.axis_size("gy").bit_length() - 1
    x_index = lax.axis_index("gx")
    y_index = lax.axis_index("gy")
    current = weights
    level_index = 0
    for bit_pos in reversed(range(x_bits)):
        own_bit = x_index >> bit_pos & 1
        current = level_step(current, angles[level_index], matrices[0], own_bit, bit_pos, True)
        level_index = level_index + 1
    for bit_pos in reversed(range(y_bits)):
        own_bit = y_index >> bit_pos & 1
        current = level_step(current, angles[level_index], matrices[1], own_bit, bit_pos, False)
        level_index = level_index + 1
    return current


def solution(mesh):
    return jax.shard_map(
        shards,
        mesh=mesh,
        in_specs=(P(("gx", "gy"), None), P(None, ("gx", "gy"), None)),
        out_specs=P(("gx", "gy"), None),
        check_vma=False,
    )
```

profile of v0, /device:TPU:1, one launch (start us, length us, event | category | flops | bytes accessed | tf_op | source)
XLA Modules:
  0.0 513.8 jit_solution(4881552665643354349)
XLA Ops:
  0.0 54.4 %slice_cosine_fusion = (f32[1,4096,128]{2,1,0:T(8,128)}, f32[1,4096,128]{2,1,0:T(8,128)S(1)}, f32[1,4096,128]{2,1,0:T(8,128)}, f32[1,4096,128]{2,1,0:T(8,128)}, ...) fusion(f32[7,4096,128]{2,1,0:T(8,128)} %param.3), kind=kLoop, calls=%fused_computation.71 | loop fusion | bytes 44040192 | tf_op jit(solution)/shard_map/cos | solution.py:44
  54.4 4.3 cos.75
  58.7 4.3 sin.43
  63.0 6.8 %multiply_add_fusion.6 = (f32[8192,64]{1,0:T(8,128)S(1)}, f32[8192,64]{1,0:T(8,128)S(1)}) fusion(f32[8192,64]{1,0:T(8,128)} %cos.75, f32[8192,64]{1,0:T(8,128)} %sin.43, f32[8192,128]{1,0:T(8,128)} %param.2), kind=kLoop, calls=%fused_computation.12 | loop fusion | flops 3145728 | bytes 12582912 | tf_op jit(solution)/shard_map/add | solution.py:47
  69.9 2.4 fusion.30
  72.5 1.4 copy-done.1
  73.9 3.6 collective-permute-start
  77.6 0.4 fusion.36
  79.2 4.3 cos.73
  83.5 4.3 sin.45
  87.8 34.8 %collective-permute-done = f32[4096,128]{1,0:T(8,128)} collective-permute-done((f32[4096,128]{1,0:T(8,128)}, f32[4096,128]{1,0:T(8,128)}, u32[]{:S(2)}, u32[]{:S(2)}) %collective-permute-start) | collective-permute-done | bytes 2097184 | tf_op jit(solution)/shard_map/ppermute | solution.py:16
  122.6 8.3 %fusion.33 = f32[4096,256]{1,0:T(8,128)} fusion(f32[128,256]{1,0:T(8,128)S(1)} %constant_dynamic-update-slice_fusion, f32[4096,128]{1,0:T(8,128)} %collective-permute-done, s32[]{:T(128)S(6)} %select_n.61, f32[8192,64]{1,0:T(8,128)} %copy-done.1, f32[8192,64]{1,0:T(8,128)} %copy-done), kind=kOutput, calls=%fused_computation.69 | convolution fusion | flops 1611661312 | bytes 10616836 | tf_op jit(solution)/shard_map/dot_general | solution.py:53
  130.9 4.8 reshape.303
  135.7 6.6 %multiply_add_fusion.5 = (f32[8192,64]{1,0:T(8,128)S(1)}, f32[8192,64]{1,0:T(8,128)S(1)}) fusion(f32[8192,64]{1,0:T(8,128)} %cos.73, f32[8192,64]{1,0:T(8,128)} %sin.45, f32[8192,128]{1,0:T(8,128)} %reshape.303), kind=kLoop, calls=%fused_computation.10 | loop fusion | flops 3145728 | bytes 12582912 | tf_op jit(solution)/shard_map/add | solution.py:47
  142.4 2.4 fusion.25
  145.1 1.2 copy-done.9
  146.3 1.8 collective-permute-start.1
  148.1 4.3 cos.71
  152.4 4.3 sin.47
  156.7 35.7 %collective-permute-done.1 = f32[4096,128]{1,0:T(8,128)} collective-permute-done((f32[4096,128]{1,0:T(8,128)}, f32[4096,128]{1,0:T(8,128)}, u32[]{:S(2)}, u32[]{:S(2)}) %collective-permute-start.1) | collective-permute-done | bytes 2097184 | tf_op jit(solution)/shard_map/ppermute | solution.py:16
  192.5 8.3 %fusion.28 = f32[4096,256]{1,0:T(8,128)} fusion(f32[128,256]{1,0:T(8,128)S(1)} %constant_dynamic-update-slice_fusion, f32[4096,128]{1,0:T(8,128)} %collective-permute-done.1, s32[]{:T(128)S(6)} %select_n.66, f32[8192,64]{1,0:T(8,128)} %copy-done.9, f32[8192,64]{1,0:T(8,128)} %copy-done.8), kind=kOutput, calls=%fused_computation.65 | convolution fusion | flops 1611661312 | bytes 10616836 | tf_op jit(solution)/shard_map/dot_general | solution.py:53
  200.7 4.8 reshape.304
  205.6 6.6 %multiply_add_fusion.4 = (f32[8192,64]{1,0:T(8,128)S(1)}, f32[8192,64]{1,0:T(8,128)S(1)}) fusion(f32[8192,64]{1,0:T(8,128)} %cos.71, f32[8192,64]{1,0:T(8,128)} %sin.47, f32[8192,128]{1,0:T(8,128)} %reshape.304), kind=kLoop, calls=%fused_computation.8 | loop fusion | flops 3145728 | bytes 12582912 | tf_op jit(solution)/shard_map/add | solution.py:47
  212.2 2.4 fusion.20
  214.9 1.2 copy-done.5
  216.1 4.1 collective-permute-start.2
  220.2 4.3 cos.69
  224.5 4.3 sin.49
  228.9 35.1 %collective-permute-done.2 = f32[4096,128]{1,0:T(8,128)} collective-permute-done((f32[4096,128]{1,0:T(8,128)}, f32[4096,128]{1,0:T(8,128)}, u32[]{:S(2)}, u32[]{:S(2)}) %collective-permute-start.2) | collective-permute-done | bytes 2097184 | tf_op jit(solution)/shard_map/ppermute | solution.py:16
  264.0 8.3 %fusion.23 = f32[4096,256]{1,0:T(8,128)} fusion(f32[128,256]{1,0:T(8,128)S(1)} %constant_dynamic-update-slice_fusion, f32[4096,128]{1,0:T(8,128)} %collective-permute-done.2, s32[]{:T(128)S(6)} %select_n.68, f32[8192,64]{1,0:T(8,128)} %copy-done.5, f32[8192,64]{1,0:T(8,128)} %copy-done.4), kind=kOutput, calls=%fused_computation.61 | convolution fusion | flops 1611661312 | bytes 10616836 | tf_op jit(solution)/shard_map/dot_general | solution.py:53
  272.3 4.8 reshape.305
  277.1 6.6 %multiply_add_fusion.3 = (f32[8192,64]{1,0:T(8,128)S(1)}, f32[8192,64]{1,0:T(8,128)S(1)}) fusion(f32[8192,64]{1,0:T(8,128)} %cos.69, f32[8192,64]{1,0:T(8,128)} %sin.49, f32[8192,128]{1,0:T(8,128)} %reshape.305), kind=kLoop, calls=%fused_computation.6 | loop fusion | flops 3145728 | bytes 12582912 | tf_op jit(solution)/shard_map/add | solution.py:47
  283.8 2.4 fusion.15
  286.4 1.2 copy-done.3
  287.7 3.4 collective-permute-start.3
  291.3 4.3 cos.67
  295.6 4.3 sin.51
  300.0 34.0 %collective-permute-done.3 = f32[4096,128]{1,0:T(8,128)} collective-permute-done((f32[4096,128]{1,0:T(8,128)}, f32[4096,128]{1,0:T(8,128)}, u32[]{:S(2)}, u32[]{:S(2)}) %collective-permute-start.3) | collective-permute-done | bytes 2097184 | tf_op jit(solution)/shard_map/ppermute | solution.py:16
  333.9 8.3 %fusion.18 = f32[4096,256]{1,0:T(8,128)} fusion(f32[128,256]{1,0:T(8,128)S(1)} %constant_dynamic-update-slice_fusion.2, f32[4096,128]{1,0:T(8,128)} %collective-permute-done.3, s32[]{:T(128)S(6)} %select_n.70, f32[8192,64]{1,0:T(8,128)} %copy-done.3, f32[8192,64]{1,0:T(8,128)} %copy-done.2), kind=kOutput, calls=%fused_computation.57 | convolution fusion | flops 1611661312 | bytes 10616836 | tf_op jit(solution)/shard_map/dot_general | solution.py:53
  342.2 4.8 reshape.306
  347.0 6.6 %multiply_add_fusion.2 = (f32[8192,64]{1,0:T(8,128)S(1)}, f32[8192,64]{1,0:T(8,128)S(1)}) fusion(f32[8192,64]{1,0:T(8,128)} %cos.67, f32[8192,64]{1,0:T(8,128)} %sin.51, f32[8192,128]{1,0:T(8,128)} %reshape.306), kind=kLoop, calls=%fused_computation.4 | loop fusion | flops 3145728 | bytes 12582912 | tf_op jit(solution)/shard_map/add | solution.py:47
  353.7 2.4 fusion.10
  356.4 1.2 copy-done.11
  357.6 1.4 collective-permute-start.4
  359.0 4.3 cos.65
  363.3 4.3 sin.53
  367.7 33.5 %collective-permute-done.4 = f32[4096,128]{1,0:T(8,128)} collective-permute-done((f32[4096,128]{1,0:T(8,128)}, f32[4096,128]{1,0:T(8,128)}, u32[]{:S(2)}, u32[]{:S(2)}) %collective-permute-start.4) | collective-permute-done | bytes 2097184 | tf_op jit(solution)/shard_map/ppermute | solution.py:16
  401.1 8.3 %fusion.13 = f32[4096,256]{1,0:T(8,128)} fusion(f32[128,256]{1,0:T(8,128)S(1)} %constant_dynamic-update-slice_fusion.2, f32[4096,128]{1,0:T(8,128)} %collective-permute-done.4, s32[]{:T(128)S(6)} %select_n.72, f32[8192,64]{1,0:T(8,128)} %copy-done.11, f32[8192,64]{1,0:T(8,128)} %copy-done.10), kind=kOutput, calls=%fused_computation.53 | convolution fusion | flops 1611661312 | bytes 10616836 | tf_op jit(solution)/shard_map/dot_general | solution.py:53
  409.4 4.8 reshape.307
  414.2 6.6 %multiply_add_fusion.1 = (f32[8192,64]{1,0:T(8,128)S(1)}, f32[8192,64]{1,0:T(8,128)S(1)}) fusion(f32[8192,64]{1,0:T(8,128)} %cos.65, f32[8192,64]{1,0:T(8,128)} %sin.53, f32[8192,128]{1,0:T(8,128)} %reshape.307), kind=kLoop, calls=%fused_computation.2 | loop fusion | flops 3145728 | bytes 12582912 | tf_op jit(solution)/shard_map/add | solution.py:47
  420.9 2.4 fusion.5
  423.6 1.2 copy-done.7
  425.0 4.3 cos.63
  429.3 2.3 sin.55
  431.6 35.7 %collective-permute-done.5 = f32[4096,128]{1,0:T(8,128)} collective-permute-done((f32[4096,128]{1,0:T(8,128)}, f32[4096,128]{1,0:T(8,128)}, u32[]{:S(2)}, u32[]{:S(2)}) %collective-permute-start.5) | collective-permute-done | bytes 2097184 | tf_op jit(solution)/shard_map/ppermute | solution.py:16
  467.3 8.3 %fusion.8 = f32[4096,256]{1,0:T(8,128)} fusion(f32[128,256]{1,0:T(8,128)S(1)} %constant_dynamic-update-slice_fusion.2, f32[4096,128]{1,0:T(8,128)} %collective-permute-done.5, s32[]{:T(128)S(6)} %select_n.74, f32[8192,64]{1,0:T(8,128)} %copy-done.7, f32[8192,64]{1,0:T(8,128)} %copy-done.6), kind=kOutput, calls=%fused_computation.49 | convolution fusion | flops 1611661312 | bytes 10616836 | tf_op jit(solution)/shard_map/dot_general | solution.py:53
  475.5 4.8 reshape.308
  480.4 6.6 %multiply_add_fusion = (f32[8192,64]{1,0:T(8,128)S(1)}, f32[8192,64]{1,0:T(8,128)S(1)}) fusion(f32[8192,64]{1,0:T(8,128)} %cos.63, f32[8192,64]{1,0:T(8,128)} %sin.55, f32[8192,128]{1,0:T(8,128)} %reshape.308), kind=kLoop, calls=%fused_computation | loop fusion | flops 3145728 | bytes 12582912 | tf_op jit(solution)/shard_map/add | solution.py:47
  487.0 2.3 fusion
  489.7 1.4 copy-done.13
  491.0 6.1 %collective-permute-start.6 = (f32[4096,128]{1,0:T(8,128)}, f32[4096,128]{1,0:T(8,128)S(1)}, u32[]{:S(2)}, u32[]{:S(2)}) collective-permute-start(f32[4096,128]{1,0:T(8,128)} %fusion), channel_id=1, source_target_pairs={{0,1},{1,0},{2,3},{3,2},{4,5},{5,4},{6,7},{7,6},{8,9},{9,8},{10,11... | collective-permute-start | bytes 6291464 | tf_op jit(solution)/shard_map/ppermute | solution.py:16
  497.2 4.0 collective-permute-done.6
  501.2 7.7 %fusion.3 = f32[4096,256]{1,0:T(8,128)} fusion(f32[128,256]{1,0:T(8,128)S(1)} %constant_dynamic-update-slice_fusion.2, f32[4096,128]{1,0:T(8,128)S(1)} %collective-permute-done.6, s32[]{:T(128)S(6)} %select_n.76, f32[8192,64]{1,0:T(8,128)} %copy-done.13, f32[8192,64]{1,0:T(8,128)} %copy-done.12), kind=kOutput, calls=%fused_computation.45 | convolution fusion | flops 1611661312 | bytes 10616836 | tf_op jit(solution)/shard_map/dot_general | solution.py:53
  508.9 4.7 reshape.309
  (42 shorter events, 3.9 us)
Async XLA Ops:
  69.9 2.6 copy-start
  69.9 4.0 copy-start.1
  73.9 48.8 %collective-permute-start = (f32[4096,128]{1,0:T(8,128)}, f32[4096,128]{1,0:T(8,128)}, u32[]{:S(2)}, u32[]{:S(2)}) collective-permute-start(f32[4096,128]{1,0:T(8,128)} %fusion.30), channel_id=1, source_target_pairs={{0,64},{64,0},{16,80},{80,16},{32,96},{96,32},{48,112},{112,48},{1... | collective-permute-start | bytes 6291464 | tf_op jit(solution)/shard_map/ppermute | solution.py:16
  142.4 2.7 copy-start.8
  142.4 3.9 copy-start.9
  146.3 46.2 %collective-permute-start.1 = (f32[4096,128]{1,0:T(8,128)}, f32[4096,128]{1,0:T(8,128)}, u32[]{:S(2)}, u32[]{:S(2)}) collective-permute-start(f32[4096,128]{1,0:T(8,128)} %fusion.25), channel_id=1, source_target_pairs={{0,32},{32,0},{16,48},{48,16},{64,96},{96,64},{80,112},{112,80},{1... | collective-permute-start | bytes 6291464 | tf_op jit(solution)/shard_map/ppermute | solution.py:16
  212.2 2.7 copy-start.4
  212.2 3.9 copy-start.5
  216.1 47.9 %collective-permute-start.2 = (f32[4096,128]{1,0:T(8,128)}, f32[4096,128]{1,0:T(8,128)}, u32[]{:S(2)}, u32[]{:S(2)}) collective-permute-start(f32[4096,128]{1,0:T(8,128)} %fusion.20), channel_id=1, source_target_pairs={{0,16},{16,0},{32,48},{48,32},{64,80},{80,64},{96,112},{112,96},{1... | collective-permute-start | bytes 6291464 | tf_op jit(solution)/shard_map/ppermute | solution.py:16
  283.7 2.7 copy-start.2
  283.8 3.9 copy-start.3
  287.7 46.3 %collective-permute-start.3 = (f32[4096,128]{1,0:T(8,128)}, f32[4096,128]{1,0:T(8,128)}, u32[]{:S(2)}, u32[]{:S(2)}) collective-permute-start(f32[4096,128]{1,0:T(8,128)} %fusion.15), channel_id=1, source_target_pairs={{0,8},{8,0},{1,9},{9,1},{2,10},{10,2},{3,11},{11,3},{4,12},{12,4},... | collective-permute-start | bytes 6291464 | tf_op jit(solution)/shard_map/ppermute | solution.py:16
  353.7 2.7 copy-start.10
  353.7 3.9 copy-start.11
  357.6 43.6 %collective-permute-start.4 = (f32[4096,128]{1,0:T(8,128)}, f32[4096,128]{1,0:T(8,128)}, u32[]{:S(2)}, u32[]{:S(2)}) collective-permute-start(f32[4096,128]{1,0:T(8,128)} %fusion.10), channel_id=1, source_target_pairs={{0,4},{4,0},{1,5},{5,1},{2,6},{6,2},{3,7},{7,3},{8,12},{12,8},{9,1... | collective-permute-start | bytes 6291464 | tf_op jit(solution)/shard_map/ppermute | solution.py:16
  420.9 2.7 copy-start.6
  420.9 3.9 copy-start.7
  424.8 42.5 %collective-permute-start.5 = (f32[4096,128]{1,0:T(8,128)}, f32[4096,128]{1,0:T(8,128)}, u32[]{:S(2)}, u32[]{:S(2)}) collective-permute-start(f32[4096,128]{1,0:T(8,128)} %fusion.5), channel_id=1, source_target_pairs={{0,2},{2,0},{1,3},{3,1},{4,6},{6,4},{5,7},{7,5},{8,10},{10,8},{9,1... | collective-permute-start | bytes 6291464 | tf_op jit(solution)/shard_map/ppermute | solution.py:16
  487.0 2.6 copy-start.12
  487.0 4.0 copy-start.13
  491.0 10.1 %collective-permute-start.6 = (f32[4096,128]{1,0:T(8,128)}, f32[4096,128]{1,0:T(8,128)S(1)}, u32[]{:S(2)}, u32[]{:S(2)}) collective-permute-start(f32[4096,128]{1,0:T(8,128)} %fusion), channel_id=1, source_target_pairs={{0,1},{1,0},{2,3},{3,2},{4,5},{5,4},{6,7},{7,6},{8,9},{9,8},{10,11... | collective-permute-start | bytes 6291464 | tf_op jit(solution)/shard_map/ppermute | solution.py:16
where the time goes:
time: 524 us; the launch traced here: 514 us
  waiting for transfers between devices  213 us (41%)
  local copies, waits for them, and re-layouts  159 us (30%)
  other arithmetic  64 us (12%)
  matrix products  57.4 us (11%)
  starting transfers between devices  20.6 us (4%)
    ppermute x7, waiting for transfers between devices, from_partner(): return lax.ppermute(block, axis, route)  213 us
    cos x8, local copies, waits for them, and re-layouts, modulate(): cosine = jnp.cos(angle_rows)  84.7 us
    dot_general x7, matrix products, interpolate(): jnp.dot(rows, level_matrix, precision=lax.Precision.HIGHEST, preferred_el...  57.4 us
    add x7, other arithmetic, modulate(): sine_part * real_part + cosine * imag_part  46.7 us
    reshape x7, local copies, waits for them, and re-layouts, level_step(): return joined.reshape(row_count, current.shape[1])  33.6 us
    sin x7, local copies, waits for them, and re-layouts, modulate(): sine_part = jnp.sin(angle_rows)  28.3 us
    ppermute x7, starting transfers between devices, from_partner(): return lax.ppermute(block, axis, route)  20.6 us
    concatenate x7, other arithmetic, modulate(): jnp.concatenate([cosine * real_part - sine_part * imag_part, sine_part *...  16.5 us
  transfers between devices with their start and end apart: 7, of which 7 were waited for; matrix products, arithmetic and copies ran while one was open for 10% of the time, Pallas kernels for 0%

commit v1 on v0

v1 whole, which is shorter than its diff:
```python
import functools
import math

import jax
import jax.numpy as jnp
import numpy as np
from jax import lax
from jax.experimental import pallas as pl
from jax.experimental.pallas import tpu as pltpu
from jax.sharding import PartitionSpec as P

MESH = pl.DeviceIdType.MESH
LEVELS = 7
CHUNK_BITS = 4
CHUNKS = 1 << CHUNK_BITS
ROWS = 4096 // CHUNKS
HALF = ROWS // 2
DEPTH = 2
SLOTS = 4
AHEAD = 3


def low_bits(level):
    return 5 - CHUNK_BITS + level


def unit_rows(level):
    return max(8, 1 << low_bits(level))


def units(level):
    return (1 << (5 + level)) // unit_rows(level)


def sel_count(level):
    return 1 << (7 - level)


def chunks_per_unit(level):
    return CHUNKS // units(level)


def series(func, degree):
    top = 3.140625**2
    nodes = (np.cos((np.arange(64) + 0.5) * np.pi / 64) + 1.0) * top / 2
    fit = np.polynomial.chebyshev.Chebyshev.fit(nodes, func(np.sqrt(nodes)), degree, domain=[0.0, top])
    return [float(np.float32(c)) for c in fit.convert(kind=np.polynomial.Polynomial).coef]


COS_COEF = series(np.cos, 6)
SIN_COEF = series(lambda r: np.sin(r) / r, 5)


def horner(coef, square):
    total = jnp.full_like(square, coef[-1])
    total = coef[-1] * square + coef[-2]
    for c in reversed(coef[:-2]):
        total = total * square + c
    return total


def cos_sin(angle):
    square = angle * angle
    return horner(COS_COEF, square), horner(SIN_COEF, square) * angle


def refine_matrices():
    nodes = np.cos((2.0 * np.arange(8) + 1.0) * math.pi / 16.0)
    sides = []
    for child in range(2):
        points = (nodes + 2.0 * child - 1.0) / 2.0
        lagrange = np.ones((8, 8))
        for j in range(8):
            for m in range(8):
                if m != j:
                    lagrange[j] *= (points - nodes[m]) / (nodes[j] - nodes[m])
        sides.append(lagrange)
    eye = np.eye(8)
    first = np.concatenate([np.kron(k, eye) for k in sides], axis=1)
    second = np.concatenate([np.kron(eye, k) for k in sides], axis=1)
    zero = np.zeros_like(first)

    def split(matrix):
        matrix = np.asarray(matrix, np.float32)
        high = matrix.astype(jnp.bfloat16)
        low = (matrix - high.astype(np.float32)).astype(jnp.bfloat16)
        return high, low

    mats = []
    for pair in (first, second):
        high, low = split(np.block([[pair, zero], [zero, pair]]))
        mats.append(np.stack([np.concatenate([high, high]), np.concatenate([low, low])]))
    last = np.zeros((256, 512))
    for slot in range(2):
        for child in range(2):
            edge = second[:, 64 * child : 64 * child + 64]
            col = 256 * slot + 128 * child
            last[64 * slot : 64 * slot + 64, col : col + 64] = edge
            last[128 + 64 * slot : 192 + 64 * slot, col + 64 : col + 128] = edge
    high, low = split(last)
    return np.stack(mats), np.stack([high, low])


def split_value(x):
    high = x.astype(jnp.bfloat16)
    low = (x - high.astype(jnp.float32)).astype(jnp.bfloat16)
    return high, low


def dot(a, b):
    return jnp.dot(a, b, preferred_element_type=jnp.float32)


def kernel(w_ref, *refs):
    p_refs = refs[:LEVELS]
    mats_ref, last_ref, out_ref = refs[LEVELS : LEVELS + 3]
    w_buf = refs[LEVELS + 3]
    p_bufs = refs[LEVELS + 4 : 2 * LEVELS + 4]
    mod, recv, staged, w_sem, p_sem, send_sem, recv_sem, out_sem = refs[2 * LEVELS + 4 :]

    gx = lax.axis_index("gx")
    gy = lax.axis_index("gy")
    own = []
    partner = []
    for level in range(LEVELS):
        if level < 3:
            weight = 1 << (2 - level)
            bit = (gx // weight) % 2
            partner.append((gx + weight - 2 * weight * bit, gy))
        else:
            weight = 1 << (6 - level)
            bit = (gy // weight) % 2
            partner.append((gx, gy + weight - 2 * weight * bit))
        own.append(bit)

    barrier = pltpu.get_barrier_semaphore()
    for device in partner:
        pl.semaphore_signal(barrier, inc=1, device_id=device, device_id_type=MESH)

    def weight_copy(unit):
        return pltpu.make_async_copy(w_ref.at[:, unit], w_buf.at[unit], w_sem.at[unit])

    def phase_copy(level, unit):
        return pltpu.make_async_copy(
            p_refs[level].at[level, :, unit], p_bufs[level].at[unit], p_sem.at[level, unit]
        )

    def exchange(level, chunk):
        slot = chunk % SLOTS
        return pltpu.make_async_remote_copy(
            src_ref=mod.at[level, slot, 1 - own[level]],
            dst_ref=recv.at[level, chunk],
            send_sem=send_sem.at[level, slot],
            recv_sem=recv_sem.at[level, chunk],
            device_id=partner[level],
            device_id_type=MESH,
        )

    def out_copy(chunk):
        return pltpu.make_async_copy(
            staged.at[chunk], out_ref.at[pl.ds(chunk * 2 * ROWS, 2 * ROWS)], out_sem.at[chunk]
        )

    def phase_rows(level, chunk, offset, count, stride):
        per = chunks_per_unit(level)
        flat = p_bufs[level].at[chunk // per].reshape(sel_count(level) * unit_rows(level), 128)
        start = (chunk % per) * (1 << low_bits(level)) + offset if per > 1 else offset
        return flat[pl.ds(start, count, stride=stride)]

    def put(level, slot, half, start, real, imag, angle):
        cosine, sine = cos_sin(angle)
        rows = pl.ds(start, real.shape[0])
        mod[level, slot, half, 0, rows] = cosine * real - sine * imag
        mod[level, slot, half, 1, rows] = sine * real + cosine * imag

    def first_stage(chunk):
        per = chunks_per_unit(0)
        unit = chunk // per
        slot = chunk % SLOTS
        flat = w_buf.at[unit].reshape(128 * 16, 128)
        left = lax.broadcasted_iota(jnp.int32, (64, 128), 1) < 64
        for u in range(1 << low_bits(0)):
            row = (chunk % per) * (1 << low_bits(0)) + u
            for half in range(2):
                even = flat[pl.ds(half * 64 * 16 + 2 * row, 64, stride=16)]
                odd = flat[pl.ds(half * 64 * 16 + 2 * row + 1, 64, stride=16)]
                real = jnp.where(left, even, pltpu.roll(odd, 64, 1))
                imag = jnp.where(left, pltpu.roll(even, 64, 1), odd)
                angle = phase_rows(0, chunk, half * 64 * 8 + u, 64, 8)
                put(0, slot, half, u * 64, real, imag, angle)

    def joined(level, chunk):
        slot = chunk % SLOTS
        both = []
        for part in range(2):
            if level == 3:
                step = HALF // 8
                pieces = []
                for s in range(8):
                    rows = pl.ds(s, step, stride=8)
                    pieces.append(
                        mod.at[level, slot, own[level], part][rows] + recv.at[level, chunk, part][rows]
                    )
                both.append(jnp.concatenate(pieces, axis=0))
            else:
                both.append(mod[level, slot, own[level], part] + recv[level, chunk, part])
        return both

    def interpolate(level, chunk):
        real, imag = joined(level, chunk)
        high, low = split_value(jnp.concatenate([real, imag], axis=0))
        wide = jnp.concatenate([high, low], axis=1)
        which = 0 if level < 3 else 1
        out = dot(wide, mats_ref[which, 0]) + dot(wide, mats_ref[which, 1])
        return out[:HALF], out[HALF:]

    def middle_stage(level, chunk):
        real, imag = interpolate(level - 1, chunk)
        slot = chunk % SLOTS
        if level <= 3:
            sel = sel_count(level)
            part = sel // 2
            stride = unit_rows(level)
            for u in range(HALF // sel):
                for i in range(2):
                    for half in range(2):
                        rows = slice(u * sel + half * part, u * sel + half * part + part)
                        lanes = slice(i * 128, i * 128 + 128)
                        angle = phase_rows(level, chunk, half * part * stride + 2 * u + i, part, stride)
                        put(level, slot, half, (2 * u + i) * part, real[rows, lanes], imag[rows, lanes], angle)
        else:
            lows = 1 << (level - 4)
            size = HALF // lows
            part = size // 2
            for half in range(2):
                for low in range(lows):
                    for i in range(2):
                        rows = slice(low * size + half * part, low * size + half * part + part)
                        lanes = slice(i * 128, i * 128 + 128)
                        angle = phase_rows(level, chunk, half * HALF + 2 * low + i, part, 2 * lows)
                        put(level, slot, half, (2 * low + i) * part, real[rows, lanes], imag[rows, lanes], angle)

    def last_stage(chunk):
        real, imag = joined(LEVELS - 1, chunk)
        high, low = split_value(jnp.concatenate([real, imag], axis=1))
        out = dot(high, last_ref[0]) + dot(low, last_ref[0]) + dot(high, last_ref[1])
        size = HALF // 8
        for low_row in range(8):
            for k in range(4):
                staged.at[chunk][pl.ds(low_row * 4 + k, size, stride=32)] = out[
                    low_row * size : low_row * size + size, k * 128 : k * 128 + 128
                ]

    def step(time, carry):
        for level in range(LEVELS):
            ahead = time + AHEAD - level * DEPTH
            per = chunks_per_unit(level)

            @pl.when((ahead >= 0) & (ahead < CHUNKS) & (ahead % per == 0))
            def _():
                phase_copy(level, ahead // per).start()
                if level == 0:
                    weight_copy(ahead // per).start()

        for stage in range(LEVELS + 1):
            chunk = time - stage * DEPTH

            @pl.when((chunk >= 0) & (chunk < CHUNKS))
            def _():
                if stage > 0:
                    exchange(stage - 1, chunk).wait_recv()
                if stage < LEVELS:
                    per = chunks_per_unit(stage)

                    @pl.when(chunk % per == 0)
                    def _():
                        phase_copy(stage, chunk // per).wait()
                        if stage == 0:
                            weight_copy(chunk // per).wait()

                    @pl.when(chunk >= SLOTS)
                    def _():
                        exchange(stage, chunk - SLOTS).wait_send()

                if stage == 0:
                    first_stage(chunk)
                elif stage < LEVELS:
                    middle_stage(stage, chunk)
                else:
                    last_stage(chunk)
                if stage == 0:

                    @pl.when(chunk == 0)
                    def _():
                        pl.semaphore_wait(barrier, LEVELS)

                if stage < LEVELS:
                    exchange(stage, chunk).start()
                else:
                    out_copy(chunk).start()

        return carry

    lax.fori_loop(-AHEAD, CHUNKS + LEVELS * DEPTH, step, 0)

    def finish(chunk, carry):
        for level in range(LEVELS):
            exchange(level, chunk).wait_send()
        return carry

    lax.fori_loop(CHUNKS - SLOTS, CHUNKS, finish, 0)

    def drain(chunk, carry):
        out_copy(chunk).wait()
        return carry

    lax.fori_loop(0, CHUNKS, drain, 0)


def shards(weights, phases):
    mats, last = refine_matrices()
    views = [
        phases.reshape(LEVELS, sel_count(level), units(level), unit_rows(level), 128)
        for level in range(LEVELS)
    ]
    anywhere = pl.BlockSpec(memory_space=pl.ANY)
    vmem = pl.BlockSpec(memory_space=pltpu.VMEM)
    scratch = [pltpu.VMEM((4, 128, 16, 128), jnp.float32)]
    scratch += [
        pltpu.VMEM((units(level), sel_count(level), unit_rows(level), 128), jnp.float32)
        for level in range(LEVELS)
    ]
    scratch += [
        pltpu.VMEM((LEVELS, SLOTS, 2, 2, HALF, 128), jnp.float32),
        pltpu.VMEM((LEVELS, CHUNKS, 2, HALF, 128), jnp.float32),
        pltpu.VMEM((CHUNKS, 2 * ROWS, 128), jnp.float32),
        pltpu.SemaphoreType.DMA((4,)),
        pltpu.SemaphoreType.DMA((LEVELS, CHUNKS)),
        pltpu.SemaphoreType.DMA((LEVELS, SLOTS)),
        pltpu.SemaphoreType.DMA((LEVELS, CHUNKS)),
        pltpu.SemaphoreType.DMA((CHUNKS,)),
    ]
    return pl.pallas_call(
        kernel,
        out_shape=jax.ShapeDtypeStruct(weights.shape, jnp.float32),
        in_specs=[anywhere] * (LEVELS + 1) + [vmem] * 2,
        out_specs=anywhere,
        scratch_shapes=scratch,
        compiler_params=pltpu.CompilerParams(
            collective_id=0, has_side_effects=True, vmem_limit_bytes=58 * 2**20
        ),
    )(weights.reshape(128, 4, 16, 128), *views, jnp.asarray(mats), jnp.asarray(last))


def solution(mesh):
    return jax.shard_map(
        shards,
        mesh=mesh,
        in_specs=(P(("gx", "gy"), None), P(None, ("gx", "gy"), None)),
        out_specs=P(("gx", "gy"), None),
        check_vma=False,
    )
```

time: 524 us -> 143 us (0.27); the launches traced: 514 us -> 142 us
  waiting for transfers between devices: 213 us -> 0 us
  local copies, waits for them, and re-layouts: 159 us -> 4.47 us
  Pallas kernels: 0 us -> 138 us
  other arithmetic: 64 us -> 0 us
  matrix products: 57.4 us -> 0 us
  starting transfers between devices: 20.6 us -> 0 us
    ppermute x7 -> x0, waiting for transfers between devices: 213 us -> none  [from_partner(): return lax.ppermute(block, axis, route)]
    pallas_call x0 -> x1, Pallas kernels: none -> 138 us  [shards(): pl.pallas_call(kernel, out_shape=jax.ShapeDtypeStruct(weights.shape, jnp....]
    cos x8 -> x0, local copies, waits for them, and re-layouts: 84.7 us -> none  [modulate(): cosine = jnp.cos(angle_rows)]
    dot_general x7 -> x0, matrix products: 57.4 us -> none  [interpolate(): jnp.dot(rows, level_matrix, precision=lax.Precision.HIGHEST, preferred_el...]
    add x7 -> x0, other arithmetic: 46.7 us -> none  [modulate(): sine_part * real_part + cosine * imag_part]
    reshape x7 -> x0, local copies, waits for them, and re-layouts: 33.6 us -> none  [level_step(): return joined.reshape(row_count, current.shape[1])]
    sin x7 -> x0, local copies, waits for them, and re-layouts: 28.3 us -> none  [modulate(): sine_part = jnp.sin(angle_rows)]
    ppermute x7 -> x0, starting transfers between devices: 20.6 us -> none  [from_partner(): return lax.ppermute(block, axis, route)]
  transfers between devices with their start and end apart: 7 -> 0, of which waited for: 7 -> 0; matrix products, arithmetic and copies ran while one was open for 10% -> 0% of each run, Pallas kernels for 0% -> 0%
where the time goes in v1:
time: 143 us; the launch traced here: 142 us
  Pallas kernels  138 us (97%)
  local copies, waits for them, and re-layouts  4.47 us (3%)
    pallas_call x1, Pallas kernels, shards(): pl.pallas_call(kernel, out_shape=jax.ShapeDtypeStruct(weights.shape, jnp....  138 us
    unnamed x1, local copies, waits for them, and re-layouts  4.47 us

profile of v1, /device:TPU:1, one launch (start us, length us, event | category | flops | bytes accessed | tf_op | source)
XLA Modules:
  0.0 142.5 jit_solution(11181156603972234820)
XLA Ops:
  0.0 138.0 %shard_map.46 = f32[8192,128]{1,0:T(8,128)} custom-call(f32[128,4,16,128]{3,2,1,0:T(8,128)} %bitcast.15, f32[7,128,4,8,128]{4,3,2,1,0:T(8,128)} %bitcast.8, f32[7,64,8,8,128]{4,3,2,1,0:T(8,128)} %bitcast.9, f32[7,32,16,8,128]{4,3,2,1,0:T(8,128)} %bitcast.10, f32[7,16,16,16,128]{4,3,2,1,0:T(8,128)} %bitcast.11, f32[7,8,16,32,128]{4,3,2,1,0:T(8,128)} %bitcast.12, ...), custom_call_target="tpu_custom_call" | custom-call | tf_op jit(solution)/shard_map/pallas_call | solution.py:343
  138.0 4.5 %copy.6 = f32[8192,128]{1,0:T(8,128)} copy(f32[8192,128]{1,0:T(8,128)} %shard_map.46) | data formatting | bytes 8388608

commit v2 on v1

v2 whole, which is shorter than its diff:
```python
import functools
import math

import jax
import jax.numpy as jnp
import numpy as np
from jax import lax
from jax.experimental import pallas as pl
from jax.experimental.pallas import tpu as pltpu
from jax.sharding import PartitionSpec as P

MESH = pl.DeviceIdType.MESH
LEVELS = 7
CHUNK_BITS = 4
CHUNKS = 1 << CHUNK_BITS
ROWS = 4096 // CHUNKS
HALF = ROWS // 2
LOW = 1 << (7 - CHUNK_BITS)
STAGES = 6
DEPTH = 2
SLOTS = 4
AHEAD = 3
LOCAL_SLOTS = 4
STATIC_SLOTS = 4
BOXES = (1, 2, 2, 4, 2, 2, 2)
PICKED = (128, 32, 16, 4, 4, 2, 1)
STAGE_OF = (0, 1, 2, 3, 3, 4, 5)
SEND_AT = (0, 0, 0, 0, 0, 0, 0)
PARTNERS = (3, 1, 3, 1, 1)


def low_bits(level):
    return 5 - CHUNK_BITS + level


def unit_rows(level):
    return max(8, 1 << low_bits(level))


def units(level):
    return (1 << (5 + level)) // unit_rows(level)


def sel_count(level):
    return 1 << (7 - level)


def chunks_per_unit(level):
    return CHUNKS // units(level)


def series(func, degree):
    top = 3.140625**2
    nodes = (np.cos((np.arange(64) + 0.5) * np.pi / 64) + 1.0) * top / 2
    fit = np.polynomial.chebyshev.Chebyshev.fit(nodes, func(np.sqrt(nodes)), degree, domain=[0.0, top])
    return [float(np.float32(c)) for c in fit.convert(kind=np.polynomial.Polynomial).coef]


COS_COEF = series(np.cos, 6)
SIN_COEF = series(lambda r: np.sin(r) / r, 5)


def horner(coef, square):
    total = jnp.full_like(square, coef[-1])
    total = coef[-1] * square + coef[-2]
    for c in reversed(coef[:-2]):
        total = total * square + c
    return total


def cos_sin(angle):
    square = angle * angle
    return horner(COS_COEF, square), horner(SIN_COEF, square) * angle


def refine_matrices():
    nodes = np.cos((2.0 * np.arange(8) + 1.0) * math.pi / 16.0)
    sides = []
    for child in range(2):
        points = (nodes + 2.0 * child - 1.0) / 2.0
        lagrange = np.ones((8, 8))
        for j in range(8):
            for m in range(8):
                if m != j:
                    lagrange[j] *= (points - nodes[m]) / (nodes[j] - nodes[m])
        sides.append(lagrange)
    eye = np.eye(8)
    first = np.concatenate([np.kron(k, eye) for k in sides], axis=1)
    second = np.concatenate([np.kron(eye, k) for k in sides], axis=1)
    zero = np.zeros_like(first)

    def split(matrix):
        matrix = np.asarray(matrix, np.float32)
        high = matrix.astype(jnp.bfloat16)
        low = (matrix - high.astype(np.float32)).astype(jnp.bfloat16)
        return high, low

    mats = []
    for pair in (first, second):
        high, low = split(np.block([[pair, zero], [zero, pair]]))
        mats.append(np.stack([np.concatenate([high, high]), np.concatenate([low, low])]))
    last = np.zeros((256, 512))
    for slot in range(2):
        for child in range(2):
            edge = second[:, 64 * child : 64 * child + 64]
            col = 256 * slot + 128 * child
            last[64 * slot : 64 * slot + 64, col : col + 64] = edge
            last[128 + 64 * slot : 192 + 64 * slot, col + 64 : col + 128] = edge
    high, low = split(last)
    return np.stack(mats), np.stack([high, low])


def split_value(x):
    high = x.astype(jnp.bfloat16)
    low = (x - high.astype(jnp.float32)).astype(jnp.bfloat16)
    return high, low


def stacked_dot(blocks, mats, which):
    high, low = split_value(jnp.concatenate(blocks, axis=0))
    wide = jnp.concatenate([high, low], axis=1)
    return dot(wide, mats[which, 0]) + dot(wide, mats[which, 1])


def turned(real, imag, angle):
    cosine, sine = cos_sin(angle)
    return cosine * real - sine * imag, sine * real + cosine * imag


def dot(a, b):
    return jnp.dot(a, b, preferred_element_type=jnp.float32)


def kernel(w_ref, *refs):
    p_refs = refs[:LEVELS]
    mats_ref, last_ref, out_ref = refs[LEVELS : LEVELS + 3]
    w_buf = refs[LEVELS + 3]
    p_bufs = refs[LEVELS + 4 : 2 * LEVELS + 4]
    held = refs[2 * LEVELS + 4 : 2 * LEVELS + 9]
    came = refs[2 * LEVELS + 9 : 2 * LEVELS + 14]
    staged, w_sem, p_sem, give_sem, get_sem, send_sem, recv_sem, out_sem = refs[2 * LEVELS + 14 :]

    gx = lax.axis_index("gx")
    gy = lax.axis_index("gy")
    x, z_high = gx // 2, gx % 2
    y, z_low, core = gy // 4, (gy // 2) % 2, gy % 2

    def flips(v):
        return (v, v + 1 - 2 * (v % 2), (v + 2) % 4, 3 - v)

    x_flips = flips(x)
    y_flips = flips(y)
    to_x = [(x_flips[j] * 2 + z_high, gy) for j in range(1, 4)]
    to_z_high = (gx + 1 - 2 * z_high, gy)
    to_y = [(gx, y_flips[j] * 4 + z_low * 2 + core) for j in range(1, 4)]
    to_z_low = (gx, gy + 2 - 4 * z_low)
    to_core = (gx, gy + 1 - 2 * core)
    level_devices = (
        [],
        [to_x[0]],
        [to_z_high],
        to_y,
        [to_y[0]],
        [to_z_low],
        [to_core],
    )
    level_picks = (
        (0,),
        (x % 2, 1 - x % 2),
        (z_high, 1 - z_high),
        y_flips,
        (y % 2, 1 - y % 2),
        (z_low, 1 - z_low),
        (core, 1 - core),
    )
    stage_devices = (to_x, [to_z_high], to_y, [to_z_low], [to_core])
    stage_picks = (x_flips, (z_high, 1 - z_high), y_flips, (z_low, 1 - z_low), (core, 1 - core))
    greeted = to_x + to_y + [to_z_high, to_z_low, to_core]

    barrier = pltpu.get_barrier_semaphore()
    for device in greeted:
        pl.semaphore_signal(barrier, inc=1, device_id=device, device_id_type=MESH)

    def weight_copy(unit):
        return pltpu.make_async_copy(w_ref.at[:, unit], w_buf.at[unit], w_sem.at[unit])

    def phase_part(level, pick, unit):
        return p_refs[level].at[level, pl.ds(pick * PICKED[level], PICKED[level]), unit]

    def phase_copy(level, unit):
        return pltpu.make_async_copy(
            phase_part(level, level_picks[level][0], unit),
            p_bufs[level].at[0, unit],
            p_sem.at[level, unit % LOCAL_SLOTS],
        )

    def phase_send(level, j, unit):
        lane = level + j - 1 + (2 if level > 3 else 0) - 1
        return pltpu.make_async_remote_copy(
            src_ref=phase_part(level, level_picks[level][j], unit),
            dst_ref=p_bufs[level].at[j, unit],
            send_sem=give_sem.at[lane, unit % STATIC_SLOTS],
            recv_sem=get_sem.at[lane, unit],
            device_id=level_devices[level][j - 1],
            device_id_type=MESH,
        )

    def held_part(stage, slot, j):
        pick = stage_picks[stage][j]
        if stage == 2:
            return held[stage].at[slot, :, pl.ds(pick * 4 * LOW, 4 * LOW)]
        if stage == 4:
            return held[stage].at[slot, :, pl.ds(pick * 8 * LOW, 8 * LOW)]
        return held[stage].at[slot, pick]

    def exchange(stage, j, chunk):
        slot = chunk % SLOTS
        lane = sum(PARTNERS[:stage]) + j - 1
        return pltpu.make_async_remote_copy(
            src_ref=held_part(stage, slot, j),
            dst_ref=came[stage].at[j - 1, chunk],
            send_sem=send_sem.at[lane, slot],
            recv_sem=recv_sem.at[lane, chunk],
            device_id=stage_devices[stage][j - 1],
            device_id_type=MESH,
        )

    def out_copy(chunk):
        return pltpu.make_async_copy(
            staged.at[chunk], out_ref.at[pl.ds(chunk * 2 * ROWS, 2 * ROWS)], out_sem.at[chunk]
        )

    def phase_rows(level, box, chunk, offset, count, stride):
        per = chunks_per_unit(level)
        flat = p_bufs[level].at[box, chunk // per].reshape(PICKED[level] * unit_rows(level), 128)
        start = (chunk % per) * (1 << low_bits(level)) + offset if per > 1 else offset
        return flat[pl.ds(start, count, stride=stride)]

    def keep(stage, slot, halves, start, real, imag):
        size = real.shape[0] // halves
        for half in range(halves):
            for part, value in enumerate((real, imag)):
                held[stage][slot, half, part, pl.ds(start, size)] = value[half * size : half * size + size]

    def own_and_came(stage, chunk):
        own = held_part(stage, chunk % SLOTS, 0)
        blocks = [own[0], own[1]]
        for j in range(PARTNERS[stage]):
            blocks += [came[stage][j, chunk, 0], came[stage][j, chunk, 1]]
        return blocks

    def first_stage(chunk):
        per = chunks_per_unit(0)
        slot = chunk % SLOTS
        flat = w_buf.at[chunk // per].reshape(128 * 16, 128)
        left = lax.broadcasted_iota(jnp.int32, (32, 128), 1) < 64
        for u in range(1 << low_bits(0)):
            row = (chunk % per) * (1 << low_bits(0)) + u
            for quarter in range(4):
                even = flat[pl.ds(quarter * 32 * 16 + 2 * row, 32, stride=16)]
                odd = flat[pl.ds(quarter * 32 * 16 + 2 * row + 1, 32, stride=16)]
                real = jnp.where(left, even, pltpu.roll(odd, 64, 1))
                imag = jnp.where(left, pltpu.roll(even, 64, 1), odd)
                angle = phase_rows(0, 0, chunk, quarter * 32 * 8 + u, 32, 8)
                real, imag = turned(real, imag, angle)
                held[0][slot, quarter, 0, pl.ds(u * 32, 32)] = real
                held[0][slot, quarter, 1, pl.ds(u * 32, 32)] = imag

    def pair_sum(out, size, rows, lanes, angles):
        total = None
        for box, angle in enumerate(angles):
            start = box * 2 * size + rows.start
            real = out[start : start + rows.stop - rows.start, lanes]
            imag = out[start + size : start + size + rows.stop - rows.start, lanes]
            value = turned(real, imag, angle)
            total = value if total is None else (total[0] + value[0], total[1] + value[1])
        return total

    def sides():
        return [(i, slice(i * 128, i * 128 + 128)) for i in range(2)]

    def second_stage(chunk):
        b = own_and_came(0, chunk)
        blocks = [b[0] + b[4], b[1] + b[5], b[2] + b[6], b[3] + b[7]]
        out = stacked_dot(blocks, mats_ref, 0)
        for u in range(LOW // 4):
            for i, lanes in sides():
                angles = [phase_rows(1, box, chunk, 2 * u + i, 32, 8) for box in range(2)]
                real, imag = pair_sum(out, HALF // 2, slice(u * 32, u * 32 + 32), lanes, angles)
                keep(1, chunk % SLOTS, 2, (2 * u + i) * 16, real, imag)

    def third_stage(chunk):
        out = stacked_dot(own_and_came(1, chunk), mats_ref, 0)
        for u in range(LOW // 2):
            for i, lanes in sides():
                angles = [phase_rows(2, box, chunk, 2 * u + i, 16, 8) for box in range(2)]
                sums = pair_sum(out, HALF // 2, slice(u * 16, u * 16 + 16), lanes, angles)
                for part in range(2):
                    held[2].at[chunk % SLOTS, part][pl.ds(2 * u + i, 16, stride=LOW)] = sums[part]

    def fourth_stage(chunk):
        size = 4 * LOW
        out = stacked_dot(own_and_came(2, chunk), mats_ref, 0)
        blocks = []
        for pair in range(2):
            parts = ([], [])
            for i, lanes in sides():
                total = None
                for box in (pair, pair + 2):
                    angle = phase_rows(3, box, chunk, i, size, 2)
                    start = box * 2 * size
                    value = turned(out[start : start + size, lanes], out[start + size : start + 2 * size, lanes], angle)
                    total = value if total is None else (total[0] + value[0], total[1] + value[1])
                parts[0].append(total[0])
                parts[1].append(total[1])
            blocks += [jnp.concatenate(p, axis=0) for p in parts]
        out = stacked_dot(blocks, mats_ref, 1)
        for i in range(2):
            for k, lanes in sides():
                angles = [phase_rows(4, box, chunk, 2 * i + k, size, 4) for box in range(2)]
                real, imag = pair_sum(out, 2 * size, slice(i * size, i * size + size), lanes, angles)
                keep(3, chunk % SLOTS, 2, (2 * i + k) * 2 * LOW, real, imag)

    def fifth_stage(chunk):
        size = 2 * LOW
        out = stacked_dot(own_and_came(3, chunk), mats_ref, 1)
        for low in range(4):
            for m, lanes in sides():
                angles = [phase_rows(5, box, chunk, 2 * low + m, size, 8) for box in range(2)]
                sums = pair_sum(out, 4 * size, slice(low * size, low * size + size), lanes, angles)
                for part in range(2):
                    held[4].at[chunk % SLOTS, part][pl.ds(2 * low + m, size, stride=8)] = sums[part]

    def last_stage(chunk):
        size = 8 * LOW
        out = stacked_dot(own_and_came(4, chunk), mats_ref, 1)
        rows = []
        for n, lanes in sides():
            angles = [phase_rows(6, box, chunk, n, size, 2) for box in range(2)]
            rows.append(jnp.concatenate(pair_sum(out, size, slice(0, size), lanes, angles), axis=1))
        high, low = split_value(jnp.concatenate(rows, axis=0))
        out = dot(high, last_ref[0]) + dot(low, last_ref[0]) + dot(high, last_ref[1])
        for n in range(2):
            for k in range(4):
                staged.at[chunk][pl.ds(n * 4 + k, size, stride=8)] = out[
                    n * size : n * size + size, k * 128 : k * 128 + 128
                ]

    stage_bodies = (first_stage, second_stage, third_stage, fourth_stage, fifth_stage, last_stage)

    def fetch(time):
        for level in range(LEVELS):
            ahead = time + AHEAD - STAGE_OF[level] * DEPTH
            per = chunks_per_unit(level)

            @pl.when((ahead >= 0) & (ahead < CHUNKS) & (ahead % per == 0))
            def _():
                phase_copy(level, ahead // per).start()
                if level == 0:
                    weight_copy(ahead // per).start()

    def give(time):
        for level in range(1, LEVELS):
            chunk = time - SEND_AT[level]
            per = chunks_per_unit(level)

            @pl.when((chunk >= 0) & (chunk < CHUNKS) & (chunk % per == 0))
            def _():
                unit = chunk // per

                @pl.when(unit >= STATIC_SLOTS)
                def _():
                    for j in range(1, BOXES[level]):
                        phase_send(level, j, unit - STATIC_SLOTS).wait_send()

                for j in range(1, BOXES[level]):
                    phase_send(level, j, unit).start()

    def work(time):
        for stage in range(STAGES):
            chunk = time - stage * DEPTH

            @pl.when((chunk >= 0) & (chunk < CHUNKS))
            def _():
                for level in range(LEVELS):
                    if STAGE_OF[level] == stage:
                        per = chunks_per_unit(level)

                        @pl.when(chunk % per == 0)
                        def _():
                            phase_copy(level, chunk // per).wait()
                            if level == 0:
                                weight_copy(chunk // per).wait()
                            for j in range(1, BOXES[level]):
                                phase_send(level, j, chunk // per).wait_recv()

                if stage > 0:
                    for j in range(1, PARTNERS[stage - 1] + 1):
                        exchange(stage - 1, j, chunk).wait_recv()
                if stage < STAGES - 1:

                    @pl.when(chunk >= SLOTS)
                    def _():
                        for j in range(1, PARTNERS[stage] + 1):
                            exchange(stage, j, chunk - SLOTS).wait_send()

                stage_bodies[stage](chunk)
                if stage < STAGES - 1:
                    for j in range(1, PARTNERS[stage] + 1):
                        exchange(stage, j, chunk).start()
                else:
                    out_copy(chunk).start()

    def early(time, carry):
        fetch(time)
        return carry

    lax.fori_loop(-AHEAD, 0, early, 0)
    pl.semaphore_wait(barrier, len(greeted))

    def step(time, carry):
        fetch(time)
        give(time)
        work(time)
        return carry

    lax.fori_loop(0, CHUNKS + (STAGES - 1) * DEPTH, step, 0)

    def finish(chunk, carry):
        for stage in range(STAGES - 1):
            for j in range(1, PARTNERS[stage] + 1):
                exchange(stage, j, chunk).wait_send()
        return carry

    lax.fori_loop(CHUNKS - SLOTS, CHUNKS, finish, 0)
    for level in range(1, LEVELS):

        def given(unit, carry):
            for j in range(1, BOXES[level]):
                phase_send(level, j, unit).wait_send()
            return carry

        lax.fori_loop(units(level) - STATIC_SLOTS, units(level), given, 0)

    def drain(chunk, carry):
        out_copy(chunk).wait()
        return carry

    lax.fori_loop(0, CHUNKS, drain, 0)


def shards(weights, phases):
    mats, last = refine_matrices()
    views = [
        phases.reshape(LEVELS, sel_count(level), units(level), unit_rows(level), 128)
        for level in range(LEVELS)
    ]
    anywhere = pl.BlockSpec(memory_space=pl.ANY)
    vmem = pl.BlockSpec(memory_space=pltpu.VMEM)

    def buffer(*shape):
        return pltpu.VMEM(shape + (128,), jnp.float32)

    scratch = [buffer(4, 128, 16)]
    scratch += [
        buffer(BOXES[level], units(level), PICKED[level], unit_rows(level)) for level in range(LEVELS)
    ]
    scratch += [
        buffer(SLOTS, 4, 2, HALF // 2),
        buffer(SLOTS, 2, 2, HALF // 2),
        buffer(SLOTS, 2, HALF),
        buffer(SLOTS, 2, 2, HALF // 2),
        buffer(SLOTS, 2, HALF),
    ]
    scratch += [
        buffer(3, CHUNKS, 2, HALF // 2),
        buffer(1, CHUNKS, 2, HALF // 2),
        buffer(3, CHUNKS, 2, HALF // 4),
        buffer(1, CHUNKS, 2, HALF // 2),
        buffer(1, CHUNKS, 2, HALF // 2),
    ]
    scratch += [
        buffer(CHUNKS, 2 * ROWS),
        pltpu.SemaphoreType.DMA((4,)),
        pltpu.SemaphoreType.DMA((LEVELS, LOCAL_SLOTS)),
        pltpu.SemaphoreType.DMA((8, STATIC_SLOTS)),
        pltpu.SemaphoreType.DMA((8, CHUNKS)),
        pltpu.SemaphoreType.DMA((9, SLOTS)),
        pltpu.SemaphoreType.DMA((9, CHUNKS)),
        pltpu.SemaphoreType.DMA((CHUNKS,)),
    ]
    return pl.pallas_call(
        kernel,
        out_shape=jax.ShapeDtypeStruct(weights.shape, jnp.float32),
        in_specs=[anywhere] * (LEVELS + 1) + [vmem] * 2,
        out_specs=anywhere,
        scratch_shapes=scratch,
        compiler_params=pltpu.CompilerParams(
            collective_id=0, has_side_effects=True, vmem_limit_bytes=58 * 2**20
        ),
    )(weights.reshape(128, 4, 16, 128), *views, jnp.asarray(mats), jnp.asarray(last))


def solution(mesh):
    return jax.shard_map(
        shards,
        mesh=mesh,
        in_specs=(P(("gx", "gy"), None), P(None, ("gx", "gy"), None)),
        out_specs=P(("gx", "gy"), None),
        check_vma=False,
    )
```

time: 143 us -> 115 us (0.80)
  Pallas kernels: 138 us -> 110 us
    pallas_call x1, Pallas kernels: 138 us -> 110 us  [shards(): pl.pallas_call(kernel, out_shape=jax.ShapeDtypeStruct(weights.shape, jnp....]
where the time goes in v2:
time: 115 us; the launch traced here: 114 us
  Pallas kernels  110 us (96%)
  local copies, waits for them, and re-layouts  4.47 us (4%)
    pallas_call x1, Pallas kernels, shards(): pl.pallas_call(kernel, out_shape=jax.ShapeDtypeStruct(weights.shape, jnp....  110 us
    unnamed x1, local copies, waits for them, and re-layouts  4.47 us

profile of v2, /device:TPU:1, one launch (start us, length us, event | category | flops | bytes accessed | tf_op | source)
XLA Modules:
  0.0 114.4 jit_solution(18338405783928704130)
XLA Ops:
  0.0 109.9 %shard_map.46 = f32[8192,128]{1,0:T(8,128)} custom-call(f32[128,4,16,128]{3,2,1,0:T(8,128)} %bitcast.15, f32[7,128,4,8,128]{4,3,2,1,0:T(8,128)} %bitcast.8, f32[7,64,8,8,128]{4,3,2,1,0:T(8,128)} %bitcast.9, f32[7,32,16,8,128]{4,3,2,1,0:T(8,128)} %bitcast.10, f32[7,16,16,16,128]{4,3,2,1,0:T(8,128)} %bitcast.11, f32[7,8,16,32,128]{4,3,2,1,0:T(8,128)} %bitcast.12, ...), custom_call_target="tpu_custom_call" | custom-call | tf_op jit(solution)/shard_map/pallas_call | solution.py:492
  109.9 4.5 %copy.6 = f32[8192,128]{1,0:T(8,128)} copy(f32[8192,128]{1,0:T(8,128)} %shard_map.46) | data formatting | bytes 8388608

commit v3 on v2

--- a/solution.py
+++ b/solution.py
@@ -11,13 +11,13 @@
 
 MESH = pl.DeviceIdType.MESH
 LEVELS = 7
-CHUNK_BITS = 4
+CHUNK_BITS = 3
 CHUNKS = 1 << CHUNK_BITS
 ROWS = 4096 // CHUNKS
 HALF = ROWS // 2
 LOW = 1 << (7 - CHUNK_BITS)
 STAGES = 6
-DEPTH = 2
+OFFSETS = (0, 2, 4, 6, 8, 9)
 SLOTS = 4
 AHEAD = 3
 LOCAL_SLOTS = 4
@@ -285,7 +285,7 @@
         out = stacked_dot(blocks, mats_ref, 0)
         for u in range(LOW // 4):
             for i, lanes in sides():
-                angles = [phase_rows(1, box, chunk, 2 * u + i, 32, 8) for box in range(2)]
+                angles = [phase_rows(1, box, chunk, 2 * u + i, 32, unit_rows(1)) for box in range(2)]
                 real, imag = pair_sum(out, HALF // 2, slice(u * 32, u * 32 + 32), lanes, angles)
                 keep(1, chunk % SLOTS, 2, (2 * u + i) * 16, real, imag)
 
@@ -293,7 +293,7 @@
         out = stacked_dot(own_and_came(1, chunk), mats_ref, 0)
         for u in range(LOW // 2):
             for i, lanes in sides():
-                angles = [phase_rows(2, box, chunk, 2 * u + i, 16, 8) for box in range(2)]
+                angles = [phase_rows(2, box, chunk, 2 * u + i, 16, unit_rows(2)) for box in range(2)]
                 sums = pair_sum(out, HALF // 2, slice(u * 16, u * 16 + 16), lanes, angles)
                 for part in range(2):
                     held[2].at[chunk % SLOTS, part][pl.ds(2 * u + i, 16, stride=LOW)] = sums[part]
@@ -350,7 +350,7 @@
 
     def fetch(time):
         for level in range(LEVELS):
-            ahead = time + AHEAD - STAGE_OF[level] * DEPTH
+            ahead = time + AHEAD - OFFSETS[STAGE_OF[level]]
             per = chunks_per_unit(level)
 
             @pl.when((ahead >= 0) & (ahead < CHUNKS) & (ahead % per == 0))
@@ -378,7 +378,7 @@
 
     def work(time):
         for stage in range(STAGES):
-            chunk = time - stage * DEPTH
+            chunk = time - OFFSETS[stage]
 
             @pl.when((chunk >= 0) & (chunk < CHUNKS))
             def _():
@@ -418,13 +418,19 @@
     lax.fori_loop(-AHEAD, 0, early, 0)
     pl.semaphore_wait(barrier, len(greeted))
 
+    def lead(time, carry):
+        give(time)
+        return carry
+
+    lax.fori_loop(min(SEND_AT), 0, lead, 0)
+
     def step(time, carry):
         fetch(time)
         give(time)
         work(time)
         return carry
 
-    lax.fori_loop(0, CHUNKS + (STAGES - 1) * DEPTH, step, 0)
+    lax.fori_loop(0, CHUNKS + OFFSETS[-1], step, 0)
 
     def finish(chunk, carry):
         for stage in range(STAGES - 1):

time: 115 us -> 109 us (0.948)
  Pallas kernels: 110 us -> 104 us
    pallas_call x1, Pallas kernels: 110 us -> 104 us  [shards(): pl.pallas_call(kernel, out_shape=jax.ShapeDtypeStruct(weights.shape, jnp....]
where the time goes in v3:
time: 109 us; the launch traced here: 108 us
  Pallas kernels  104 us (95%)
  local copies, waits for them, and re-layouts  4.47 us (4%)
    pallas_call x1, Pallas kernels, shards(): pl.pallas_call(kernel, out_shape=jax.ShapeDtypeStruct(weights.shape, jnp....  104 us
    unnamed x1, local copies, waits for them, and re-layouts  4.47 us

profile of v3, /device:TPU:1, one launch (start us, length us, event | category | flops | bytes accessed | tf_op | source)
XLA Modules:
  0.0 108.5 jit_solution(16530763899697963539)
XLA Ops:
  0.0 104.0 %shard_map.46 = f32[8192,128]{1,0:T(8,128)} custom-call(f32[128,4,16,128]{3,2,1,0:T(8,128)} %bitcast.15, f32[7,128,4,8,128]{4,3,2,1,0:T(8,128)} %bitcast.8, f32[7,64,8,8,128]{4,3,2,1,0:T(8,128)} %bitcast.9, f32[7,32,8,16,128]{4,3,2,1,0:T(8,128)} %bitcast.10, f32[7,16,8,32,128]{4,3,2,1,0:T(8,128)} %bitcast.11, f32[7,8,8,64,128]{4,3,2,1,0:T(8,128)} %bitcast.12, ...), custom_call_target="tpu_custom_call" | custom-call | tf_op jit(solution)/shard_map/pallas_call | solution.py:498
  104.0 4.5 %copy.6 = f32[8192,128]{1,0:T(8,128)} copy(f32[8192,128]{1,0:T(8,128)} %shard_map.46) | data formatting | bytes 8388608

commit v4 on v3

--- a/solution.py
+++ b/solution.py
@@ -20,6 +20,7 @@
 OFFSETS = (0, 2, 4, 6, 8, 9)
 SLOTS = 4
 AHEAD = 3
+PIECES = 8
 LOCAL_SLOTS = 4
 STATIC_SLOTS = 4
 BOXES = (1, 2, 2, 4, 2, 2, 2)
@@ -455,6 +456,23 @@
     lax.fori_loop(0, CHUNKS, drain, 0)
 
 
+def hand_on(in_ref, out_ref, held, in_sem, out_sem):
+    size = out_ref.shape[0] // PIECES
+    reads = []
+    writes = []
+    for k in range(PIECES):
+        rows = pl.ds(k * size, size)
+        reads.append(pltpu.make_async_copy(in_ref.at[rows], held.at[rows], in_sem.at[k]))
+        writes.append(pltpu.make_async_copy(held.at[rows], out_ref.at[rows], out_sem.at[k]))
+    for read in reads:
+        read.start()
+    for read, write in zip(reads, writes):
+        read.wait()
+        write.start()
+    for write in writes:
+        write.wait()
+
+
 def shards(weights, phases):
     mats, last = refine_matrices()
     views = [
@@ -495,7 +513,7 @@
         pltpu.SemaphoreType.DMA((9, CHUNKS)),
         pltpu.SemaphoreType.DMA((CHUNKS,)),
     ]
-    return pl.pallas_call(
+    result = pl.pallas_call(
         kernel,
         out_shape=jax.ShapeDtypeStruct(weights.shape, jnp.float32),
         in_specs=[anywhere] * (LEVELS + 1) + [vmem] * 2,
@@ -505,6 +523,17 @@
             collective_id=0, has_side_effects=True, vmem_limit_bytes=58 * 2**20
         ),
     )(weights.reshape(128, 4, 16, 128), *views, jnp.asarray(mats), jnp.asarray(last))
+    return pl.pallas_call(
+        hand_on,
+        out_shape=jax.ShapeDtypeStruct(weights.shape, jnp.float32),
+        in_specs=[anywhere],
+        out_specs=anywhere,
+        scratch_shapes=[
+            buffer(*weights.shape[:1]),
+            pltpu.SemaphoreType.DMA((PIECES,)),
+            pltpu.SemaphoreType.DMA((PIECES,)),
+        ],
+    )(result)
 
 
 def solution(mesh):

time: 109 us -> 108 us (level)
  local copies, waits for them, and re-layouts: 4.47 us -> 0 us
  Pallas kernels: 104 us -> 108 us
    unnamed x1 -> x0, local copies, waits for them, and re-layouts: 4.47 us -> none
    pallas_call x0 -> x1, Pallas kernels: none -> 3.58 us  [shards(): pl.pallas_call(hand_on, out_shape=jax.ShapeDtypeStruct(weights.shape, jnp...]
where the time goes in v4:
time: 108 us
  Pallas kernels  108 us (100%)
    pallas_call x1, Pallas kernels, shards(): pl.pallas_call(kernel, out_shape=jax.ShapeDtypeStruct(weights.shape, jnp....  104 us
    pallas_call x1, Pallas kernels, shards(): pl.pallas_call(hand_on, out_shape=jax.ShapeDtypeStruct(weights.shape, jnp...  3.58 us

profile of v4, /device:TPU:1, one launch (start us, length us, event | category | flops | bytes accessed | tf_op | source)
XLA Modules:
  0.0 107.6 jit_solution(16584584123924537727)
XLA Ops:
  0.0 104.0 %shard_map.46.in_ref = f32[8192,128]{1,0:T(8,128)} custom-call(f32[128,4,16,128]{3,2,1,0:T(8,128)} %bitcast.15, f32[7,128,4,8,128]{4,3,2,1,0:T(8,128)} %bitcast.8, f32[7,64,8,8,128]{4,3,2,1,0:T(8,128)} %bitcast.9, f32[7,32,8,16,128]{4,3,2,1,0:T(8,128)} %bitcast.10, f32[7,16,8,32,128]{4,3,2,1,0:T(8,128)} %bitcast.11, f32[7,8,8,64,128]{4,3,2,1,0:T(8,128)} %bitcast.12, ...), custom_call_target="tpu_custom_call" | custom-call | tf_op jit(solution)/shard_map/pallas_call | solution.py:516
  104.0 3.6 %shard_map.47 = f32[8192,128]{1,0:T(8,128)} custom-call(f32[8192,128]{1,0:T(8,128)} %shard_map.46.in_ref), custom_call_target="tpu_custom_call" | custom-call | tf_op jit(solution)/shard_map/pallas_call | solution.py:526

commit v5 on v4

--- a/solution.py
+++ b/solution.py
@@ -17,7 +17,7 @@
 HALF = ROWS // 2
 LOW = 1 << (7 - CHUNK_BITS)
 STAGES = 6
-OFFSETS = (0, 2, 4, 6, 8, 9)
+OFFSETS = (0, 2, 4, 6, 8, 10)
 SLOTS = 4
 AHEAD = 3
 PIECES = 8
@@ -26,7 +26,7 @@
 BOXES = (1, 2, 2, 4, 2, 2, 2)
 PICKED = (128, 32, 16, 4, 4, 2, 1)
 STAGE_OF = (0, 1, 2, 3, 3, 4, 5)
-SEND_AT = (0, 0, 0, 0, 0, 0, 0)
+SEND_AT = (0, 0, -1, 0, 0, -2, 0)
 PARTNERS = (3, 1, 3, 1, 1)
 
 

time: 108 us -> 108 us (level)
  no operation moved by 1% of the time
where the time goes in v5:
time: 108 us
  Pallas kernels  108 us (100%)
    pallas_call x1, Pallas kernels, shards(): pl.pallas_call(kernel, out_shape=jax.ShapeDtypeStruct(weights.shape, jnp....  104 us
    pallas_call x1, Pallas kernels, shards(): pl.pallas_call(hand_on, out_shape=jax.ShapeDtypeStruct(weights.shape, jnp...  3.58 us

profile of v5, /device:TPU:1, one launch (start us, length us, event | category | flops | bytes accessed | tf_op | source)
XLA Modules:
  0.0 107.6 jit_solution(13024038286889865310)
XLA Ops:
  0.0 104.0 %shard_map.46.in_ref = f32[8192,128]{1,0:T(8,128)} custom-call(f32[128,4,16,128]{3,2,1,0:T(8,128)} %bitcast.15, f32[7,128,4,8,128]{4,3,2,1,0:T(8,128)} %bitcast.8, f32[7,64,8,8,128]{4,3,2,1,0:T(8,128)} %bitcast.9, f32[7,32,8,16,128]{4,3,2,1,0:T(8,128)} %bitcast.10, f32[7,16,8,32,128]{4,3,2,1,0:T(8,128)} %bitcast.11, f32[7,8,8,64,128]{4,3,2,1,0:T(8,128)} %bitcast.12, ...), custom_call_target="tpu_custom_call" | custom-call | tf_op jit(solution)/shard_map/pallas_call | solution.py:516
  104.0 3.6 %shard_map.47 = f32[8192,128]{1,0:T(8,128)} custom-call(f32[8192,128]{1,0:T(8,128)} %shard_map.46.in_ref), custom_call_target="tpu_custom_call" | custom-call | tf_op jit(solution)/shard_map/pallas_call | solution.py:526
